TPU v7x, 128 devices: a whole 4x4x4 slice. The times are simulated.
128 devices in a mesh: row: 8 (over y_lo, z), col: 16 (over x, y_hi, core).
Axes of the slice: x: 4, y: 4 (y_hi: 2, y_lo: 2; y = y_hi * 2 + y_lo), z: 4, core: 2. Of those that a mesh axis runs over, the one named last changes fastest.
Arguments:
- amplitudes: float32 [512, 20480], P('row', 'col'), may hold values from -6 to 6
- integrals: float32 [512, 38400], P('col', 'row'), may hold values from -0.25 to 0.25
Outputs:
- residual: float32 [38400, 20480], P('row', 'col')
All inputs are finite; a program needn't handle non-finite values.
Results may differ from a plain program's by a relative error of at most 0.00007.
Values sent between devices are 32-bit elements; how exact they have to be, the bound alone decides.
No kernel may reach another device: no remote copies, remote signals or barrier semaphores. Data moves between devices by JAX's collectives and lax.ppermute only.
A program may use at most 128 MiB of HBM per device.

v0:
```python
import jax
import jax.numpy as jnp
from jax import lax
from jax.sharding import PartitionSpec as P


def contract_rows(left_block, right_block):
    return lax.dot_general(
        left_block,
        right_block,
        (((0,), (0,)), ((), ())),
        precision=lax.Precision.HIGHEST,
        preferred_element_type=jnp.float32,
    )


def ladder(amps_block, integral_block):
    whole_amps = lax.all_gather(amps_block, "row", axis=0, tiled=True)
    return contract_rows(lax.all_gather(integral_block, "col", axis=0, tiled=True), whole_amps)


def body(amplitudes, integrals):
    return 0.5 * ladder(amplitudes, integrals)


def solution(mesh):
    in_specs = (P("row", "col"), P("col", "row"))
    out_specs = P("row", "col")
    return jax.shard_map(body, mesh=mesh, in_specs=in_specs, out_specs=out_specs, check_vma=False)
```

profile of v0, /device:TPU:1, one launch (start us, length us, event | category | flops | bytes accessed | tf_op | source)
XLA Modules:
  0.0 227.3 jit_solution(12496698475896982546)
XLA Ops:
  6.5 0.0 all-gather.5.cloned.1.call-start
  6.5 0.7 all-gather.5.cloned.1.call-update
  7.3 0.0 all-gather.3.cloned.1.call-start
  7.3 0.7 all-gather.3.cloned.1.call-update
  8.0 42.6 %all-gather.5.cloned.1.call-done = f32[512,1280]{1,0:T(8,128)} async-done(((f32[64,1280]{1,0:T(8,128)}), f32[512,1280]{1,0:T(8,128)}) %all-gather.5.cloned.1.call-update) | async-done | bytes 2621456 | tf_op jit(solution)/shard_map/all_gather | solution.py:18
  50.6 85.5 %all-gather.3.cloned.1.call-done = f32[512,4800]{1,0:T(8,128)} async-done(((f32[32,4800]{1,0:T(8,128)}), f32[512,4800]{1,0:T(8,128)}) %all-gather.3.cloned.1.call-update) | async-done | bytes 9830416 | tf_op jit(solution)/shard_map/all_gather | solution.py:19
  136.0 84.5 %convolution_multiply_fusion = f32[4800,1280]{1,0:T(8,128)} fusion(f32[512,4800]{1,0:T(8,128)} %all-gather.3.cloned.1.call-done, f32[512,1280]{1,0:T(8,128)} %all-gather.5.cloned.1.call-done), kind=kOutput, calls=%fused_computation | convolution fusion | flops 37754880000 | bytes 37027840 | tf_op jit(solution)/shard_map/dot_general | solution.py:8
Async XLA Ops:
  6.5 44.0 %all-gather.5.cloned.1.call-start = ((), (), s32[]{:S(2)}) async-start(), calls=%async_computation.1 | async-start | bytes 2949120 | tf_op jit(solution)/shard_map/all_gather | solution.py:18
  7.3 128.8 %all-gather.3.cloned.1.call-start = ((), (), s32[]{:S(2)}) async-start(), calls=%async_computation | async-start | bytes 10584064 | tf_op jit(solution)/shard_map/all_gather | solution.py:19
Sparse Core Ops, SparseCore 0:
  9.0 41.5 all-gather.4
  53.0 83.0 all-gather.2
where the time goes:
time: 227 us
  waiting for transfers between devices  129 us (57%)
  matrix products  84.5 us (37%)
  between operations  13.4 us (6%)
    all_gather x1, waiting for transfers between devices, ladder(): lax.all_gather(integral_block, 'col', axis=0, tiled=True)  85.5 us
    dot_general x1, matrix products, contract_rows(): lax.dot_general(left_block, right_block, (((0,), (0,)), ((), ())), precis...  84.5 us
    all_gather x1, waiting for transfers between devices, ladder(): whole_amps = lax.all_gather(amps_block, 'row', axis=0, tiled=True)  42.6 us
  transfers between devices with their start and end apart: 2, of which 2 were waited for; matrix products, arithmetic and copies ran while one was open for 0% of the time, Pallas kernels for 0%

commit v1 on v0

--- a/solution.py
+++ b/solution.py
@@ -15,7 +15,9 @@
 
 
 def ladder(amps_block, integral_block):
-    whole_amps = lax.all_gather(amps_block, "row", axis=0, tiled=True)
+    whole_amps = jnp.concatenate(
+        lax.all_to_all(jnp.stack([amps_block] * lax.axis_size("row")), "row", 0, 0), axis=0
+    )
     return contract_rows(lax.all_gather(integral_block, "col", axis=0, tiled=True), whole_amps)
 
 

time: 227 us -> 152 us (0.67)
  waiting for transfers between devices: 129 us -> 47.1 us
  blocking collectives: 0 us -> 44.4 us
  matrix products: 84.5 us -> 45.9 us
    all_to_all x0 -> x1, blocking collectives: none -> 44.4 us  [ladder(): lax.all_to_all(jnp.stack([amps_block] * lax.axis_size('row')), 'row', 0, 0)]
    all_gather x1 -> x0, waiting for transfers between devices: 42.6 us -> none  [ladder(): whole_amps = lax.all_gather(amps_block, 'row', axis=0, tiled=True)]
    all_gather x1, waiting for transfers between devices: 85.5 us -> 46.4 us  [ladder(): lax.all_gather(integral_block, 'col', axis=0, tiled=True)]
    dot_general x1, matrix products: 84.5 us -> 45.9 us  [contract_rows(): lax.dot_general(left_block, right_block, (((0,), (0,)), ((), ())), precis...]
  transfers between devices with their start and end apart: 2 -> 1, of which waited for: 2 -> 1; matrix products, arithmetic and copies ran while one was open for 0% -> 1% of each run, Pallas kernels for 0% -> 0%
where the time goes in v1:
time: 152 us
  waiting for transfers between devices  47.1 us (31%)
  matrix products  45.9 us (30%)
  blocking collectives  44.4 us (29%)
  between operations  13.4 us (9%)
    all_gather x1, waiting for transfers between devices, ladder(): lax.all_gather(integral_block, 'col', axis=0, tiled=True)  46.4 us
    dot_general x1, matrix products, contract_rows(): lax.dot_general(left_block, right_block, (((0,), (0,)), ((), ())), precis...  45.9 us
    all_to_all x1, blocking collectives, ladder(): lax.all_to_all(jnp.stack([amps_block] * lax.axis_size('row')), 'row', 0, 0)  44.4 us
  transfers between devices with their start and end apart: 1, of which 1 were waited for; matrix products, arithmetic and copies ran while one was open for 1% of the time, Pallas kernels for 0%

profile of v1, /device:TPU:1, one launch (start us, length us, event | category | flops | bytes accessed | tf_op | source)
XLA Modules:
  0.0 152.0 jit_solution(2585463985937343268)
XLA Ops:
  6.5 0.0 all-gather.2.cloned.1.call-start
  6.5 0.7 all-gather.2.cloned.1.call-update
  7.3 1.2 stack.2
  8.4 44.4 %all_to_all.5 = f32[8,64,1280]{2,1,0:T(8,128)S(1)} all-to-all(f32[8,64,1280]{2,1,0:T(8,128)S(1)} %stack.2), channel_id=1, replica_groups=mesh['row'=8,'col'=16] {'row'}, dimensions={0} | all-to-all | bytes 5242880 | tf_op jit(solution)/shard_map/all_to_all | solution.py:19
  52.9 46.4 %all-gather.2.cloned.1.call-done = f32[512,4800]{1,0:T(8,128)} async-done(((f32[32,4800]{1,0:T(8,128)}), f32[512,4800]{1,0:T(8,128)}) %all-gather.2.cloned.1.call-update) | async-done | bytes 9830416 | tf_op jit(solution)/shard_map/all_gather | solution.py:21
  99.2 45.9 %convolution_multiply_fusion = f32[4800,1280]{1,0:T(8,128)} fusion(f32[512,4800]{1,0:T(8,128)} %all-gather.2.cloned.1.call-done, f32[512,1280]{1,0:T(8,128)S(1)} %bitcast.3), kind=kOutput, calls=%fused_computation | convolution fusion | flops 37754880000 | bytes 37027840 | tf_op jit(solution)/shard_map/dot_general | solution.py:8
Async XLA Ops:
  6.5 92.7 %all-gather.2.cloned.1.call-start = ((), (), s32[]{:S(2)}) async-start(), calls=%async_computation.1 | async-start | bytes 10584064 | tf_op jit(solution)/shard_map/all_gather | solution.py:21
Sparse Core Ops, SparseCore 0:
  9.8 89.4 all-gather.1
